TPU v7x, 256 devices: a whole 4x4x8 slice. The times are simulated.
256 devices in a mesh: dp: 8 (over y, core), shard: 32 (over z, x).
Axes of the slice: x: 4, y: 4, z: 8, core: 2. Of those that a mesh axis runs over, the one named last changes fastest.
Arguments:
- grads: bfloat16 [104, 1024, 704], P(None, 'shard'), may hold values from -150 to 150
- momentum: bfloat16 [256, 1024, 704], P(('dp', 'shard')), may hold values from -24 to 24
- owners: int32 [104], replicated, may hold values from 0 to 255, as said below
Outputs:
- updates: bfloat16 [104, 1024, 704], P(None, 'shard')
- momentum_next: bfloat16 [256, 1024, 704], P(('dp', 'shard'))
Inputs may be any that keep to these rules, and one draw needn't show every extreme that they name: `owners`: device d is the one with dp index d // 32 and shard index d % 32. Each device owns at most 1 matrices, and some device owns exactly 1.
All inputs are finite; a program needn't handle non-finite values.
Results may differ from a plain program's by a relative error of at most 0.0058.
Values may be sent and summed in bfloat16 or wider, within the bound.
No kernel may reach another device: no remote copies, remote signals or barrier semaphores. Data moves between devices by JAX's collectives and lax.ppermute only.
A program may use at most 128 MiB of HBM per device.

v0:
```python
import functools
import math

import jax
import jax.numpy as jnp
from jax import lax
from jax.experimental import pallas as pl
from jax.experimental.pallas import tpu as pltpu
from jax.sharding import PartitionSpec as P

DECAY = 0.95
LINEAR, CUBIC, QUINTIC = 3.4445, -4.775, 2.0315
EPS = 1e-07
ITERS = 2
AXES = ("dp", "shard")
NZ, NX, NC, NY = 8, 4, 2, 4
SHARDS = NZ * NX
RING = NC * SHARDS
NT = (((1,), (1,)), ((), ()))
NN = (((1,), (0,)), ((), ()))
ANY = pl.BlockSpec(memory_space=pl.ANY)
HBM = pl.BlockSpec(memory_space=pltpu.HBM)
SMEM = pl.BlockSpec(memory_space=pltpu.SMEM)
VMEM = pl.BlockSpec(memory_space=pltpu.VMEM)


def seat(z, x):
    pick = jnp.where if isinstance(z, jax.Array) else (lambda c, a, b: a if c else b)
    return pick(z < NZ // 2, 2 * z, 2 * NZ - 1 - 2 * z) + NZ * pick(x < NX // 2, 2 * x, 2 * NX - 1 - 2 * x)


SEATED = sorted(range(SHARDS), key=lambda s: seat(s // NX, s % NX))
GROUPS_32 = [[g * SHARDS + s for s in SEATED] for g in range(NY * NC)]
GROUPS_64 = [[y * RING + c * SHARDS + s for c in range(NC) for s in SEATED] for y in range(NY)]


def hop_y(array, step):
    count = NY * RING
    return lax.ppermute(array, AXES, [(d, (d + RING * step) % count) for d in range(count)])


def hop_core(array):
    return lax.ppermute(array, AXES, [(d, d ^ SHARDS) for d in range(NY * RING)])


LANES = 128


def put_dense(out, index, block):
    n, columns = block.shape
    whole = columns // LANES
    for tile in range(whole):
        out[index, tile * n : (tile + 1) * n] = block[:, tile * LANES : (tile + 1) * LANES]
    rest = block[:, whole * LANES :]
    out[index, whole * n :] = jnp.concatenate([rest[: n // 2], rest[n // 2 :]], axis=1)


def get_dense(blocks, index, n):
    whole = blocks.shape[1] // n
    tiles = [blocks[index, tile * n : (tile + 1) * n] for tile in range(whole)]
    rest = blocks[index, whole * n :]
    return tiles + [jnp.concatenate([rest[:, : LANES // 2], rest[:, LANES // 2 :]], axis=0)]


def dense_rows(n, columns):
    return n * columns // LANES


def pack_kernel(owners, group, grads, out, rows, places, sems):
    count, unroll = owners.shape[0], 8

    def copy(m, k):
        return pltpu.make_async_copy(grads.at[m], rows.at[k], sems.at[k])

    def look(m, found):
        owner = owners[m]
        mine = (owner >> 5) == group[0]

        @pl.when(mine)
        def _():
            copy(m, found).start()
            places[found] = seat((owner >> 2) & (NZ - 1), owner & (NX - 1))

        return found + mine.astype(jnp.int32)

    def look_many(i, found):
        for j in range(unroll):
            found = look(i * unroll + j, found)
        return found

    found = lax.fori_loop(0, count // unroll, look_many, jnp.int32(0))
    for m in range(count // unroll * unroll, count):
        found = look(m, found)

    def store(k, carry):
        copy(0, k).wait()
        put_dense(out, places[k], rows[k])
        return carry

    lax.fori_loop(0, found, store, 0)


def pack(owners, group, grads):
    _, rows, columns = grads.shape
    return pl.pallas_call(
        pack_kernel,
        out_shape=jax.ShapeDtypeStruct((SHARDS, dense_rows(rows, columns), LANES), grads.dtype),
        in_specs=[SMEM, SMEM, HBM],
        out_specs=VMEM,
        scratch_shapes=[
            pltpu.VMEM((SHARDS, rows, columns), grads.dtype),
            pltpu.SMEM((SHARDS,), jnp.int32),
            pltpu.SemaphoreType.DMA((SHARDS,)),
        ],
        compiler_params=pltpu.CompilerParams(vmem_limit_bytes=56 * 2**20),
        name="pack_rows",
    )(owners, group, grads)


def dot(a, b, dims):
    return lax.dot_general(a, b, dims, preferred_element_type=jnp.float32)


def step_kernel(scale, owned_ref, rows_ref, mom_ref, out_ref, next_ref, blend, cur, gram, poly):
    rows = mom_ref.shape[1] // SHARDS
    half = rows // NC
    span = NX * rows
    owned = owned_ref[0] > 0
    total = jnp.zeros((8, span), jnp.float32)
    for z in range(NZ):
        cols = slice(z * span, (z + 1) * span)
        tiles = zip(*[get_dense(rows_ref, seat(z, x), rows) for x in range(NX)])
        grad = jnp.concatenate([jnp.concatenate(tile, axis=0) for tile in tiles], axis=1)
        grad = jnp.where(owned, grad.T.astype(jnp.float32), 0.0)
        renewed = DECAY * mom_ref[:, cols].astype(jnp.float32) + grad
        next_ref[:, cols] = renewed.astype(jnp.bfloat16)
        mixed = grad + DECAY * renewed
        blend[:, cols] = mixed
        total = total + jnp.sum((mixed * mixed).reshape(-1, 8, span), axis=0)
    inverse = 1.0 / (jnp.sqrt(jnp.sum(total)) + EPS)
    cur[...] = (blend[...] * inverse).astype(jnp.bfloat16)
    columns, total_rows = cur.shape
    cuts = [(low, min(low + 256, columns)) for low in range(0, columns, 256)]
    wide = 2 * span
    for iteration in range(ITERS):
        for low, high in cuts:
            block = dot(cur[:high], cur[low:high], NT).astype(jnp.bfloat16)
            gram[:high, low:high] = block
            if low:
                gram[low:high, :low] = block[:low].T
        for low, high in cuts:
            square = dot(gram[:high], gram[:, low:high], NN)
            block = (CUBIC * gram[:high, low:high].astype(jnp.float32) + QUINTIC * square).astype(jnp.bfloat16)
            poly[:high, low:high] = block
            if low:
                poly[low:high, :low] = block[:low].T
        factor = poly[...]
        if iteration + 1 < ITERS:
            x = cur[...]
            cur[...] = (LINEAR * x.astype(jnp.float32) + dot(factor, x, NN)).astype(jnp.bfloat16)
            continue
        for left in range(0, total_rows, wide):
            x = cur[:, left : left + wide]
            last = (scale * LINEAR) * x.astype(jnp.float32) + scale * dot(factor, x, NN)
            last = last.astype(jnp.bfloat16)
            for z in range(left // span, (left + wide) // span):
                update = last[:, z * span - left : (z + 1) * span - left].T
                for x in range(NX):
                    for c in range(NC):
                        low = x * rows + c * half
                        out_ref[c * SHARDS + seat(z, x)] = update[low : low + half]


def muon_step(owned, rows, momentum_t):
    columns, total_rows = momentum_t.shape
    scale = 0.2 * math.sqrt(max(columns, total_rows))
    square = pltpu.VMEM((columns, columns), jnp.bfloat16)
    return pl.pallas_call(
        functools.partial(step_kernel, scale),
        out_shape=(
            jax.ShapeDtypeStruct((RING, total_rows // RING, columns), jnp.bfloat16),
            jax.ShapeDtypeStruct(momentum_t.shape, jnp.bfloat16),
        ),
        in_specs=[SMEM, VMEM, VMEM],
        out_specs=(VMEM, VMEM),
        scratch_shapes=[
            pltpu.VMEM(momentum_t.shape, jnp.float32),
            pltpu.VMEM(momentum_t.shape, jnp.bfloat16),
            square,
            square,
        ],
        compiler_params=pltpu.CompilerParams(vmem_limit_bytes=48 * 2**20),
        name="newton_schulz",
    )(owned, rows, momentum_t)


def select_kernel(seats, order, counts, where, blocks, out):
    y = where[0]

    def body(k, carry):
        out[k] = blocks[seats[order[y * RING + k]]]
        return carry

    lax.fori_loop(0, counts[y], body, 0)


def select(seats, order, counts, where, blocks, slots):
    return pl.pallas_call(
        select_kernel,
        out_shape=jax.ShapeDtypeStruct((slots,) + blocks.shape[1:], blocks.dtype),
        in_specs=[SMEM] * 4 + [VMEM],
        out_specs=VMEM,
        compiler_params=pltpu.CompilerParams(vmem_limit_bytes=16 * 2**20),
        name="select_blocks",
    )(seats, order, counts, where, blocks)


def place_kernel(origins, order, counts, where, *refs):
    pieces, out, sems = refs[: len(origins)], refs[-2], refs[-1]
    y, c = where[0], where[1]
    half = out.shape[1] // NC
    for run in ("start", "wait"):
        for (core, hop, first), piece in zip(origins, pieces):
            low = pl.multiple_of((c ^ core) * half, half)
            home = (y + hop) & (NY - 1)

            def body(k, carry):
                m = order[home * RING + k]
                copy = pltpu.make_async_copy(
                    piece.at[k - first], out.at[m, pl.ds(low, half)], sems.at[core, m]
                )
                getattr(copy, run)()
                return carry

            def four(i, carry):
                for j in range(4):
                    body(first + 4 * i + j, 0)
                return carry

            last = jnp.minimum(counts[home], first + piece.shape[0])
            fours = jnp.maximum(last - first, 0) >> 2
            lax.fori_loop(0, fours, four, 0)
            lax.fori_loop(first + 4 * fours, last, body, 0)


def place(origins, order, counts, where, pieces, count, base=None):
    _, half, columns = pieces[0].shape
    bases = [] if base is None else [base]
    return pl.pallas_call(
        functools.partial(place_kernel, origins),
        out_shape=jax.ShapeDtypeStruct((count, NC * half, columns), pieces[0].dtype),
        in_specs=[SMEM] * 3 + [VMEM] * len(pieces) + [HBM] * len(bases),
        out_specs=HBM,
        input_output_aliases={3 + len(pieces): 0} if bases else {},
        scratch_shapes=[pltpu.SemaphoreType.DMA((NC, count))],
        compiler_params=pltpu.CompilerParams(vmem_limit_bytes=16 * 2**20),
        name="place_blocks",
    )(order, counts, where, *pieces, *bases)


def spread(slots, seats, order, counts, where, blocks):
    count = seats.shape[0]
    split = slots // 2
    own = select(seats, order, counts, where, blocks, slots)
    low, high = own[:split], own[split:]
    below_low, above_high = hop_y(low, 1), hop_y(high, -1)
    below_high, above_low = hop_y(high, 1), hop_y(low, -1)
    far = [hop_y(below_low, 1), hop_y(above_high, -1)]
    early = [own, below_low, above_high]
    early += [hop_core(piece) for piece in early]
    origins = [(core, *origin) for core in range(NC) for origin in ((0, 0), (3, 0), (1, split))]
    updates = place(origins, order, counts, where, early, count)
    late = lax.optimization_barrier([below_high, above_low] + far)
    late += [hop_core(piece) for piece in late]
    origins = [(core, *origin) for core in range(NC) for origin in ((3, split), (1, 0), (2, 0), (2, split))]
    return place(origins, order, counts, where, late, count, updates)


def on_device(grads, momentum, owners):
    count = owners.shape[0]
    group = lax.axis_index("dp")
    me = lax.axis_index(AXES)
    where = jnp.stack([me // RING, me // SHARDS % NC]).astype(jnp.int32)
    packed = pack(owners, group[None].astype(jnp.int32), grads)
    rows = lax.all_to_all(packed, AXES, 0, 0, tiled=True, axis_index_groups=GROUPS_32)

    ids = jnp.arange(count, dtype=jnp.int32)
    homes = owners // RING
    seats = (owners & SHARDS) + seat((owners >> 2) & (NZ - 1), owners & (NX - 1))
    before = (homes[:, None] == homes[None, :]) & (owners[None, :] < owners[:, None])
    slot = homes * RING + jnp.sum(before.astype(jnp.int32), axis=1)
    order = jnp.sum(
        jnp.where(slot[None, :] == jnp.arange(NY * RING, dtype=jnp.int32)[:, None], ids[None, :], 0), axis=1
    )
    counts = jnp.sum((homes[None, :] == jnp.arange(NY, dtype=jnp.int32)[:, None]).astype(jnp.int32), axis=1)
    owned = jnp.any(owners == me)[None].astype(jnp.int32)

    blocks, following = muon_step(owned, rows, momentum[0].T)
    blocks = lax.all_to_all(blocks, AXES, 0, 0, tiled=True, axis_index_groups=GROUPS_64)
    few = 34
    updates = lax.cond(
        jnp.max(counts) <= few,
        functools.partial(spread, few),
        functools.partial(spread, RING),
        seats,
        order,
        counts,
        where,
        blocks,
    )
    return (updates, following.T[None])


def solution(mesh):
    return jax.shard_map(
        on_device,
        mesh=mesh,
        in_specs=(P(None, "shard", None), P(AXES, None, None), P()),
        out_specs=(P(None, "shard", None), P(AXES, None, None)),
        check_vma=False,
    )
```

profile of v0, /device:TPU:33, one launch (start us, length us, event | category | flops | bytes accessed | tf_op | source)
XLA Modules:
  0.0 149.0 jit_solution(8011017184636976368)
XLA Ops:
  0.6 3.9 %pack_rows.1 = bf16[32,176,128]{2,1,0:T(8,128)(2,1)} custom-call(s32[104]{0:T(128)} %owners.1, s32[1]{0:T(128)} %bitcast.3.group, bf16[104,32,704]{2,1,0:T(8,128)(2,1)} %grads.1), custom_call_target="tpu_custom_call" | custom-call | tf_op jit(solution)/shard_map/pack_rows/pallas_call | solution.py:105
  4.5 10.8 %all-to-all-start = ((bf16[32,176,128]{2,1,0:T(8,128)(2,1)}), bf16[32,176,128]{2,1,0:T(8,128)(2,1)S(1)}, u32[]{:S(2)}, u32[]{:S(2)}) async-start(bf16[32,176,128]{2,1,0:T(8,128)(2,1)} %pack_rows.1), calls=%async_computation | async-start | bytes 2883584 | tf_op jit(solution)/shard_map/all_to_all | solution.py:285
  15.3 0.6 compare_reduce_fusion
  16.6 35.6 %all-to-all-done.rows_ref = bf16[32,176,128]{2,1,0:T(8,128)(2,1)S(1)} async-done(((bf16[32,176,128]{2,1,0:T(8,128)(2,1)}), bf16[32,176,128]{2,1,0:T(8,128)(2,1)S(1)}, u32[]{:S(2)}, u32[]{:S(2)}) %all-to-all-start) | async-done | bytes 1441824 | tf_op jit(solution)/shard_map/all_to_all | solution.py:285
  52.2 8.3 %newton_schulz.1 = (bf16[64,16,704]{2,1,0:T(8,128)(2,1)}, bf16[704,1024]{1,0:T(8,128)(2,1)}) custom-call(s32[1]{0:T(128)} %bitcast.2.owned_ref, bf16[32,176,128]{2,1,0:T(8,128)(2,1)S(1)} %all-to-all-done.rows_ref, bf16[704,1024]{1,0:T(8,128)(2,1)S(1)} %bitcast.10), custom_call_target="tpu_custom_call" | custom-call | tf_op jit(solution)/shard_map/newton_schulz/pallas_call | solution.py:178
  60.5 6.6 %all-to-all-start.1 = ((bf16[64,16,704]{2,1,0:T(8,128)(2,1)}), bf16[64,16,704]{2,1,0:T(8,128)(2,1)S(1)}, u32[]{:S(2)}, u32[]{:S(2)}) async-start(bf16[64,16,704]{2,1,0:T(8,128)(2,1)} %get-tuple-element.45), calls=%async_computation.1 | async-start | bytes 3145728 | tf_op jit(solution)/shard_map/all_to_all | solution.py:299
  67.1 0.1 convert_reduce_fusion.1
  67.2 0.7 reduce_max.9
  68.6 0.1 pad_add_fusion
  68.7 0.2 convert_reduce_fusion
  68.8 0.1 select_reduce_fusion
  69.0 38.2 %all-to-all-done.1 = bf16[64,16,704]{2,1,0:T(8,128)(2,1)S(1)} async-done(((bf16[64,16,704]{2,1,0:T(8,128)(2,1)}), bf16[64,16,704]{2,1,0:T(8,128)(2,1)S(1)}, u32[]{:S(2)}, u32[]{:S(2)}) %all-to-all-start.1) | async-done | bytes 1441824 | tf_op jit(solution)/shard_map/all_to_all | solution.py:299
  107.2 41.7 %conditional.1 = (bf16[104,32,704]{2,1,0:T(8,128)(2,1)}) conditional(s32[]{:T(128)} %convert_element_type.15, (s32[104]{0:T(128)S(1)}, s32[256]{0:T(256)S(1)}, s32[4]{0:T(128)S(1)}, s32[2]{0:T(128)S(1)}, bf16[64,16,704]{2,1,0:T(8,128)(2,1)S(1)}) %tuple.16, (s32[104]{0:T(128)S(1)}, s32[256]{0:T(256)S(1)}, s32[4]{0:T(128)S(1)}, s32[2]{0:T(128)S(1)}, ...), branch_computations={%region_5.6_spmd, %region_6.7_spmd} | conditional | bytes 43254288 | solution.py:301
  107.2 0.8 select_blocks.3.refs_0_
  108.0 0.1 fusion.4
  108.1 2.1 %collective-permute-start.15 = (bf16[17,16,704]{2,1,0:T(8,128)(2,1)S(1)}, bf16[17,16,704]{2,1,0:T(8,128)(2,1)S(1)}, u32[]{:S(2)}, u32[]{:S(2)}) collective-permute-start(bf16[17,16,704]{2,1,0:T(8,128)(2,1)S(1)} %get-tuple-element.49), channel_id=1, source_target_pairs={{0,64},{1,65},{2,66},{3,67},{4,68},{5,69},{6,70},{7,71},{8,72},{9,... | collective-permute-start | bytes 1148936 | tf_op jit(solution)/shard_map/cond/branch_1_fun/ppermute | solution.py:39
  110.2 1.1 collective-permute-start.17
  111.3 0.3 collective-permute-start.13
  111.6 2.4 %collective-permute-start.14 = (bf16[17,16,704]{2,1,0:T(8,128)(2,1)S(1)}, bf16[17,16,704]{2,1,0:T(8,128)(2,1)S(1)}, u32[]{:S(2)}, u32[]{:S(2)}) collective-permute-start(bf16[17,16,704]{2,1,0:T(8,128)(2,1)S(1)} %get-tuple-element.49), channel_id=1, source_target_pairs={{0,192},{1,193},{2,194},{3,195},{4,196},{5,197},{6,198},{7,199},{8... | collective-permute-start | bytes 1148936 | tf_op jit(solution)/shard_map/cond/branch_1_fun/ppermute | solution.py:39
  114.0 7.2 %collective-permute-done.15.refs_1_ = bf16[17,16,704]{2,1,0:T(8,128)(2,1)S(1)} collective-permute-done((bf16[17,16,704]{2,1,0:T(8,128)(2,1)S(1)}, bf16[17,16,704]{2,1,0:T(8,128)(2,1)S(1)}, u32[]{:S(2)}, u32[]{:S(2)}) %collective-permute-start.15) | collective-permute-done | bytes 383008 | tf_op jit(solution)/shard_map/cond/branch_1_fun/ppermute | solution.py:39
  121.2 0.2 collective-permute-start.16
  121.4 2.5 %collective-permute-start.18 = (bf16[17,16,704]{2,1,0:T(8,128)(2,1)S(1)}, bf16[17,16,704]{2,1,0:T(8,128)(2,1)S(1)}, u32[]{:S(2)}, u32[]{:S(2)}) collective-permute-start(bf16[17,16,704]{2,1,0:T(8,128)(2,1)S(1)} %collective-permute-done.17.refs_2_), channel_id=1, source_target_pairs={{0,192},{1,193},{2,194},{3,195},{4,196},{5,197},{6,198},{7,199},{8... | collective-permute-start | bytes 1148936 | tf_op jit(solution)/shard_map/cond/branch_1_fun/ppermute | solution.py:39
  123.9 1.4 collective-permute-start.23
  125.3 4.8 %collective-permute-done.13.refs_0_ = bf16[17,16,704]{2,1,0:T(8,128)(2,1)S(1)} collective-permute-done((bf16[17,16,704]{2,1,0:T(8,128)(2,1)S(1)}, bf16[17,16,704]{2,1,0:T(8,128)(2,1)S(1)}, u32[]{:S(2)}, u32[]{:S(2)}) %collective-permute-start.13) | collective-permute-done | bytes 383008 | tf_op jit(solution)/shard_map/cond/branch_1_fun/ppermute | solution.py:39
  130.2 0.9 collective-permute-start.24
  131.0 0.9 collective-permute-start.25
  132.0 7.2 %collective-permute-done.16.refs_2_ = bf16[17,16,704]{2,1,0:T(8,128)(2,1)S(1)} collective-permute-done((bf16[17,16,704]{2,1,0:T(8,128)(2,1)S(1)}, bf16[17,16,704]{2,1,0:T(8,128)(2,1)S(1)}, u32[]{:S(2)}, u32[]{:S(2)}) %collective-permute-start.16) | collective-permute-done | bytes 383008 | tf_op jit(solution)/shard_map/cond/branch_1_fun/ppermute | solution.py:39
  139.1 1.0 collective-permute-start.19
  140.2 0.5 collective-permute-start.21
  140.7 0.1 collective-permute-start.22
  140.8 4.0 %place_blocks.6.refs_8_ = bf16[104,32,704]{2,1,0:T(8,128)(2,1)} custom-call(s32[256]{0:T(256)S(1)} %get-tuple-element.32.order, s32[4]{0:T(128)S(1)} %get-tuple-element.33.counts, s32[2]{0:T(128)S(1)} %get-tuple-element.34.where, bf16[34,16,704]{2,1,0:T(8,128)(2,1)S(1)} %select_blocks.3.refs_0_, bf16[17,16,704]{2,1,0:T(8,128)(2,1)S(1)} %collective-permute-done.15.refs_1_, ...), custom_call_target="tpu_custom_call" | custom-call | tf_op jit(solution)/shard_map/cond/branch_1_fun/place_blocks/pallas_call | solution.py:249
  144.8 4.0 %place_blocks.7 = bf16[104,32,704]{2,1,0:T(8,128)(2,1)} custom-call(s32[256]{0:T(256)S(1)} %get-tuple-element.32.order, s32[4]{0:T(128)S(1)} %get-tuple-element.33.counts, s32[2]{0:T(128)S(1)} %get-tuple-element.34.where, bf16[17,16,704]{2,1,0:T(8,128)(2,1)S(1)} %collective-permute-done.13.refs_0_, ...), custom_call_target="tpu_custom_call", output_to_operand_aliasing={{}: (11, {})} | custom-call | tf_op jit(solution)/shard_map/cond/branch_1_fun/place_blocks/pallas_call | solution.py:249
  (17 shorter events, 0.1 us)
Async XLA Ops:
  4.5 10.8 %copy-start.1 = (s32[104]{0:T(128)S(1)}, s32[104]{0:T(128)}, u32[]{:S(2)}) copy-start(s32[104]{0:T(128)} %owners.1) | copy-start | bytes 1252
  4.5 47.7 %copy-start = (bf16[1,1024,704]{1,2,0:T(8,128)(2,1)S(1)}, bf16[1,1024,704]{1,2,0:T(8,128)(2,1)}, u32[]{:S(2)}) copy-start(bf16[1,1024,704]{1,2,0:T(8,128)(2,1)} %param.6) | copy-start | bytes 4325380
  4.5 47.7 %all-to-all-start = ((bf16[32,176,128]{2,1,0:T(8,128)(2,1)}), bf16[32,176,128]{2,1,0:T(8,128)(2,1)S(1)}, u32[]{:S(2)}, u32[]{:S(2)}) async-start(bf16[32,176,128]{2,1,0:T(8,128)(2,1)} %pack_rows.1), calls=%async_computation | async-start | bytes 2883584 | tf_op jit(solution)/shard_map/all_to_all | solution.py:285
  60.5 46.7 %all-to-all-start.1 = ((bf16[64,16,704]{2,1,0:T(8,128)(2,1)}), bf16[64,16,704]{2,1,0:T(8,128)(2,1)S(1)}, u32[]{:S(2)}, u32[]{:S(2)}) async-start(bf16[64,16,704]{2,1,0:T(8,128)(2,1)} %get-tuple-element.45), calls=%async_computation.1 | async-start | bytes 3145728 | tf_op jit(solution)/shard_map/all_to_all | solution.py:299
  108.1 13.1 %collective-permute-start.15 = (bf16[17,16,704]{2,1,0:T(8,128)(2,1)S(1)}, bf16[17,16,704]{2,1,0:T(8,128)(2,1)S(1)}, u32[]{:S(2)}, u32[]{:S(2)}) collective-permute-start(bf16[17,16,704]{2,1,0:T(8,128)(2,1)S(1)} %get-tuple-element.49), channel_id=1, source_target_pairs={{0,64},{1,65},{2,66},{3,67},{4,68},{5,69},{6,70},{7,71},{8,72},{9,... | collective-permute-start | bytes 1148936 | tf_op jit(solution)/shard_map/cond/branch_1_fun/ppermute | solution.py:39
  110.2 11.2 %collective-permute-start.17 = (bf16[17,16,704]{2,1,0:T(8,128)(2,1)S(1)}, bf16[17,16,704]{2,1,0:T(8,128)(2,1)S(1)}, u32[]{:S(2)}, u32[]{:S(2)}) collective-permute-start(bf16[17,16,704]{2,1,0:T(8,128)(2,1)S(1)} %get-tuple-element.50), channel_id=1, source_target_pairs={{0,192},{1,193},{2,194},{3,195},{4,196},{5,197},{6,198},{7,199},{8... | collective-permute-start | bytes 1148936 | tf_op jit(solution)/shard_map/cond/branch_1_fun/ppermute | solution.py:39
  111.3 18.8 %collective-permute-start.13 = (bf16[17,16,704]{2,1,0:T(8,128)(2,1)S(1)}, bf16[17,16,704]{2,1,0:T(8,128)(2,1)S(1)}, u32[]{:S(2)}, u32[]{:S(2)}) collective-permute-start(bf16[17,16,704]{2,1,0:T(8,128)(2,1)S(1)} %get-tuple-element.50), channel_id=1, source_target_pairs={{0,64},{1,65},{2,66},{3,67},{4,68},{5,69},{6,70},{7,71},{8,72},{9,... | collective-permute-start | bytes 1148936 | tf_op jit(solution)/shard_map/cond/branch_1_fun/ppermute | solution.py:39
  111.6 19.4 %collective-permute-start.14 = (bf16[17,16,704]{2,1,0:T(8,128)(2,1)S(1)}, bf16[17,16,704]{2,1,0:T(8,128)(2,1)S(1)}, u32[]{:S(2)}, u32[]{:S(2)}) collective-permute-start(bf16[17,16,704]{2,1,0:T(8,128)(2,1)S(1)} %get-tuple-element.49), channel_id=1, source_target_pairs={{0,192},{1,193},{2,194},{3,195},{4,196},{5,197},{6,198},{7,199},{8... | collective-permute-start | bytes 1148936 | tf_op jit(solution)/shard_map/cond/branch_1_fun/ppermute | solution.py:39
  121.2 17.9 %collective-permute-start.16 = (bf16[17,16,704]{2,1,0:T(8,128)(2,1)S(1)}, bf16[17,16,704]{2,1,0:T(8,128)(2,1)S(1)}, u32[]{:S(2)}, u32[]{:S(2)}) collective-permute-start(bf16[17,16,704]{2,1,0:T(8,128)(2,1)S(1)} %collective-permute-done.15.refs_1_), channel_id=1, source_target_pairs={{0,64},{1,65},{2,66},{3,67},{4,68},{5,69},{6,70},{7,71},{8,72},{9,... | collective-permute-start | bytes 1148936 | tf_op jit(solution)/shard_map/cond/branch_1_fun/ppermute | solution.py:39
  121.4 17.7 %collective-permute-start.18 = (bf16[17,16,704]{2,1,0:T(8,128)(2,1)S(1)}, bf16[17,16,704]{2,1,0:T(8,128)(2,1)S(1)}, u32[]{:S(2)}, u32[]{:S(2)}) collective-permute-start(bf16[17,16,704]{2,1,0:T(8,128)(2,1)S(1)} %collective-permute-done.17.refs_2_), channel_id=1, source_target_pairs={{0,192},{1,193},{2,194},{3,195},{4,196},{5,197},{6,198},{7,199},{8... | collective-permute-start | bytes 1148936 | tf_op jit(solution)/shard_map/cond/branch_1_fun/ppermute | solution.py:39
  123.9 16.9 %collective-permute-start.23 = (bf16[34,16,704]{2,1,0:T(8,128)(2,1)S(1)}, bf16[34,16,704]{2,1,0:T(8,128)(2,1)S(1)}, u32[]{:S(2)}, u32[]{:S(2)}) collective-permute-start(bf16[34,16,704]{2,1,0:T(8,128)(2,1)S(1)} %select_blocks.3.refs_0_), channel_id=1, source_target_pairs={{0,32},{1,33},{2,34},{3,35},{4,36},{5,37},{6,38},{7,39},{8,40},{9,... | collective-permute-start | bytes 2297864 | tf_op jit(solution)/shard_map/cond/branch_1_fun/ppermute | solution.py:43
  130.2 10.0 %collective-permute-start.24 = (bf16[17,16,704]{2,1,0:T(8,128)(2,1)S(1)}, bf16[17,16,704]{2,1,0:T(8,128)(2,1)S(1)}, u32[]{:S(2)}, u32[]{:S(2)}) collective-permute-start(bf16[17,16,704]{2,1,0:T(8,128)(2,1)S(1)} %collective-permute-done.15.refs_1_), channel_id=1, source_target_pairs={{0,32},{1,33},{2,34},{3,35},{4,36},{5,37},{6,38},{7,39},{8,40},{9,... | collective-permute-start | bytes 1148936 | tf_op jit(solution)/shard_map/cond/branch_1_fun/ppermute | solution.py:43
  131.0 9.6 %collective-permute-start.25 = (bf16[17,16,704]{2,1,0:T(8,128)(2,1)S(1)}, bf16[17,16,704]{2,1,0:T(8,128)(2,1)S(1)}, u32[]{:S(2)}, u32[]{:S(2)}) collective-permute-start(bf16[17,16,704]{2,1,0:T(8,128)(2,1)S(1)} %collective-permute-done.17.refs_2_), channel_id=1, source_target_pairs={{0,32},{1,33},{2,34},{3,35},{4,36},{5,37},{6,38},{7,39},{8,40},{9,... | collective-permute-start | bytes 1148936 | tf_op jit(solution)/shard_map/cond/branch_1_fun/ppermute | solution.py:43
  139.1 5.7 %collective-permute-start.19 = (bf16[17,16,704]{2,1,0:T(8,128)(2,1)S(1)}, bf16[17,16,704]{2,1,0:T(8,128)(2,1)S(1)}, u32[]{:S(2)}, u32[]{:S(2)}) collective-permute-start(bf16[17,16,704]{2,1,0:T(8,128)(2,1)S(1)} %collective-permute-done.13.refs_0_), channel_id=1, source_target_pairs={{0,32},{1,33},{2,34},{3,35},{4,36},{5,37},{6,38},{7,39},{8,40},{9,... | collective-permute-start | bytes 1148936 | tf_op jit(solution)/shard_map/cond/branch_1_fun/ppermute | solution.py:43
  140.1 4.7 %collective-permute-start.20 = (bf16[17,16,704]{2,1,0:T(8,128)(2,1)S(1)}, bf16[17,16,704]{2,1,0:T(8,128)(2,1)S(1)}, u32[]{:S(2)}, u32[]{:S(2)}) collective-permute-start(bf16[17,16,704]{2,1,0:T(8,128)(2,1)S(1)} %collective-permute-done.14.refs_1_), channel_id=1, source_target_pairs={{0,32},{1,33},{2,34},{3,35},{4,36},{5,37},{6,38},{7,39},{8,40},{9,... | collective-permute-start | bytes 1148936 | tf_op jit(solution)/shard_map/cond/branch_1_fun/ppermute | solution.py:43
  140.2 4.7 %collective-permute-start.21 = (bf16[17,16,704]{2,1,0:T(8,128)(2,1)S(1)}, bf16[17,16,704]{2,1,0:T(8,128)(2,1)S(1)}, u32[]{:S(2)}, u32[]{:S(2)}) collective-permute-start(bf16[17,16,704]{2,1,0:T(8,128)(2,1)S(1)} %collective-permute-done.16.refs_2_), channel_id=1, source_target_pairs={{0,32},{1,33},{2,34},{3,35},{4,36},{5,37},{6,38},{7,39},{8,40},{9,... | collective-permute-start | bytes 1148936 | tf_op jit(solution)/shard_map/cond/branch_1_fun/ppermute | solution.py:43
  140.7 4.2 %collective-permute-start.22 = (bf16[17,16,704]{2,1,0:T(8,128)(2,1)S(1)}, bf16[17,16,704]{2,1,0:T(8,128)(2,1)S(1)}, u32[]{:S(2)}, u32[]{:S(2)}) collective-permute-start(bf16[17,16,704]{2,1,0:T(8,128)(2,1)S(1)} %collective-permute-done.18.refs_3_), channel_id=1, source_target_pairs={{0,32},{1,33},{2,34},{3,35},{4,36},{5,37},{6,38},{7,39},{8,40},{9,... | collective-permute-start | bytes 1148936 | tf_op jit(solution)/shard_map/cond/branch_1_fun/ppermute | solution.py:43
where the time goes:
time: 150 us; the launch traced here: 149 us
  waiting for transfers between devices  93 us (62%)
  starting transfers between devices  30.8 us (21%)
  Pallas kernels  21 us (14%)
  between operations  2.22 us (1%)
  other arithmetic  1.82 us (1%)
    all_to_all x1, waiting for transfers between devices, on_device(): lax.all_to_all(blocks, AXES, 0, 0, tiled=True, axis_index_groups=GROUPS_64)  38.2 us
    all_to_all x1, waiting for transfers between devices, on_device(): lax.all_to_all(packed, AXES, 0, 0, tiled=True, axis_index_groups=GROUPS_32)  35.6 us
    ppermute x6, waiting for transfers between devices, hop_y(): lax.ppermute(array, AXES, [(d, (d + RING * step) % count) for d in range(...  19.2 us
    all_to_all x1, starting transfers between devices, on_device(): lax.all_to_all(packed, AXES, 0, 0, tiled=True, axis_index_groups=GROUPS_32)  10.8 us
    ppermute x6, starting transfers between devices, hop_y(): lax.ppermute(array, AXES, [(d, (d + RING * step) % count) for d in range(...  8.6 us
    pallas_call x1, Pallas kernels, muon_step(): pl.pallas_call(functools.partial(step_kernel, scale), out_shape=(jax.Shap...  8.33 us
    pallas_call x2, Pallas kernels, place(): pl.pallas_call(functools.partial(place_kernel, origins), out_shape=jax.Sh...  8.03 us
    all_to_all x1, starting transfers between devices, on_device(): lax.all_to_all(blocks, AXES, 0, 0, tiled=True, axis_index_groups=GROUPS_64)  6.55 us
  transfers between devices with their start and end apart: 15, of which 5 were waited for; matrix products, arithmetic and copies ran while one was open for 1% of the time, Pallas kernels for 3%

commit v1 on v0

--- a/solution.py
+++ b/solution.py
@@ -15,7 +15,7 @@
 AXES = ("dp", "shard")
 NZ, NX, NC, NY = 8, 4, 2, 4
 SHARDS = NZ * NX
-RING = NC * SHARDS
+GROUPS = NY * NC
 NT = (((1,), (1,)), ((), ()))
 NN = (((1,), (0,)), ((), ()))
 ANY = pl.BlockSpec(memory_space=pl.ANY)
@@ -30,17 +30,16 @@
 
 
 SEATED = sorted(range(SHARDS), key=lambda s: seat(s // NX, s % NX))
-GROUPS_32 = [[g * SHARDS + s for s in SEATED] for g in range(NY * NC)]
-GROUPS_64 = [[y * RING + c * SHARDS + s for c in range(NC) for s in SEATED] for y in range(NY)]
+MEMBERS = [[g * SHARDS + s for s in SEATED] for g in range(GROUPS)]
 
 
 def hop_y(array, step):
-    count = NY * RING
-    return lax.ppermute(array, AXES, [(d, (d + RING * step) % count) for d in range(count)])
+    count, along = GROUPS * SHARDS, NC * SHARDS
+    return lax.ppermute(array, AXES, [(d, (d + along * step) % count) for d in range(count)])
 
 
 def hop_core(array):
-    return lax.ppermute(array, AXES, [(d, d ^ SHARDS) for d in range(NY * RING)])
+    return lax.ppermute(array, AXES, [(d, d ^ SHARDS) for d in range(GROUPS * SHARDS)])
 
 
 LANES = 128
@@ -123,7 +122,6 @@
 
 def step_kernel(scale, owned_ref, rows_ref, mom_ref, out_ref, next_ref, blend, cur, gram, poly):
     rows = mom_ref.shape[1] // SHARDS
-    half = rows // NC
     span = NX * rows
     owned = owned_ref[0] > 0
     total = jnp.zeros((8, span), jnp.float32)
@@ -166,9 +164,7 @@
             for z in range(left // span, (left + wide) // span):
                 update = last[:, z * span - left : (z + 1) * span - left].T
                 for x in range(NX):
-                    for c in range(NC):
-                        low = x * rows + c * half
-                        out_ref[c * SHARDS + seat(z, x)] = update[low : low + half]
+                    put_dense(out_ref, seat(z, x), update[x * rows : (x + 1) * rows])
 
 
 def muon_step(owned, rows, momentum_t):
@@ -178,7 +174,7 @@
     return pl.pallas_call(
         functools.partial(step_kernel, scale),
         out_shape=(
-            jax.ShapeDtypeStruct((RING, total_rows // RING, columns), jnp.bfloat16),
+            jax.ShapeDtypeStruct(rows.shape, jnp.bfloat16),
             jax.ShapeDtypeStruct(momentum_t.shape, jnp.bfloat16),
         ),
         in_specs=[SMEM, VMEM, VMEM],
@@ -195,13 +191,13 @@
 
 
 def select_kernel(seats, order, counts, where, blocks, out):
-    y = where[0]
+    group = where[0]
 
     def body(k, carry):
-        out[k] = blocks[seats[order[y * RING + k]]]
+        out[k] = blocks[seats[order[group * SHARDS + k]]]
         return carry
 
-    lax.fori_loop(0, counts[y], body, 0)
+    lax.fori_loop(0, counts[group], body, 0)
 
 
 def select(seats, order, counts, where, blocks, slots):
@@ -216,19 +212,30 @@
 
 
 def place_kernel(origins, order, counts, where, *refs):
-    pieces, out, sems = refs[: len(origins)], refs[-2], refs[-1]
-    y, c = where[0], where[1]
-    half = out.shape[1] // NC
+    pieces, (out, rows, sems) = refs[: len(origins)], refs[-3:]
+    height = out.shape[1]
+    offsets = [sum(piece.shape[0] for piece in pieces[:i]) for i in range(len(pieces))]
+
+    def unpack(chosen, k, carry):
+        for i in chosen:
+            for tile, value in enumerate(get_dense(pieces[i], k, height)):
+                left = tile * LANES
+                rows[offsets[i] + k, :, left : left + value.shape[1]] = value
+        return carry
+
+    done = 0
+    for size in sorted({piece.shape[0] for piece in pieces}):
+        chosen = [i for i, piece in enumerate(pieces) if piece.shape[0] >= size]
+        lax.fori_loop(done, size, functools.partial(unpack, chosen), 0)
+        done = size
+
     for run in ("start", "wait"):
-        for (core, hop, first), piece in zip(origins, pieces):
-            low = pl.multiple_of((c ^ core) * half, half)
-            home = (y + hop) & (NY - 1)
+        for (core, hop, first), piece, offset in zip(origins, pieces, offsets):
+            home = (where[0] ^ core) + NC * hop & (GROUPS - 1)
 
             def body(k, carry):
-                m = order[home * RING + k]
-                copy = pltpu.make_async_copy(
-                    piece.at[k - first], out.at[m, pl.ds(low, half)], sems.at[core, m]
-                )
+                m = order[home * SHARDS + k]
+                copy = pltpu.make_async_copy(rows.at[offset + k - first], out.at[m], sems.at[m])
                 getattr(copy, run)()
                 return carry
 
@@ -243,24 +250,26 @@
             lax.fori_loop(first + 4 * fours, last, body, 0)
 
 
-def place(origins, order, counts, where, pieces, count, base=None):
-    _, half, columns = pieces[0].shape
+def place(origins, order, counts, where, pieces, shape, base=None):
     bases = [] if base is None else [base]
+    slots = sum(piece.shape[0] for piece in pieces)
     return pl.pallas_call(
         functools.partial(place_kernel, origins),
-        out_shape=jax.ShapeDtypeStruct((count, NC * half, columns), pieces[0].dtype),
+        out_shape=jax.ShapeDtypeStruct(shape, pieces[0].dtype),
         in_specs=[SMEM] * 3 + [VMEM] * len(pieces) + [HBM] * len(bases),
         out_specs=HBM,
         input_output_aliases={3 + len(pieces): 0} if bases else {},
-        scratch_shapes=[pltpu.SemaphoreType.DMA((NC, count))],
+        scratch_shapes=[
+            pltpu.VMEM((slots,) + shape[1:], pieces[0].dtype),
+            pltpu.SemaphoreType.DMA((shape[0],)),
+        ],
         compiler_params=pltpu.CompilerParams(vmem_limit_bytes=16 * 2**20),
         name="place_blocks",
     )(order, counts, where, *pieces, *bases)
 
 
-def spread(slots, seats, order, counts, where, blocks):
-    count = seats.shape[0]
-    split = slots // 2
+def spread(slots, shape, seats, order, counts, where, blocks):
+    split = (slots + 1) // 2
     own = select(seats, order, counts, where, blocks, slots)
     low, high = own[:split], own[split:]
     below_low, above_high = hop_y(low, 1), hop_y(high, -1)
@@ -269,39 +278,39 @@
     early = [own, below_low, above_high]
     early += [hop_core(piece) for piece in early]
     origins = [(core, *origin) for core in range(NC) for origin in ((0, 0), (3, 0), (1, split))]
-    updates = place(origins, order, counts, where, early, count)
+    updates = place(origins, order, counts, where, early, shape)
     late = lax.optimization_barrier([below_high, above_low] + far)
     late += [hop_core(piece) for piece in late]
     origins = [(core, *origin) for core in range(NC) for origin in ((3, split), (1, 0), (2, 0), (2, split))]
-    return place(origins, order, counts, where, late, count, updates)
+    return place(origins, order, counts, where, late, shape, updates)
 
 
 def on_device(grads, momentum, owners):
     count = owners.shape[0]
     group = lax.axis_index("dp")
     me = lax.axis_index(AXES)
-    where = jnp.stack([me // RING, me // SHARDS % NC]).astype(jnp.int32)
-    packed = pack(owners, group[None].astype(jnp.int32), grads)
-    rows = lax.all_to_all(packed, AXES, 0, 0, tiled=True, axis_index_groups=GROUPS_32)
+    where = group[None].astype(jnp.int32)
+    packed = pack(owners, where, grads)
+    rows = lax.all_to_all(packed, AXES, 0, 0, tiled=True, axis_index_groups=MEMBERS)
 
     ids = jnp.arange(count, dtype=jnp.int32)
-    homes = owners // RING
-    seats = (owners & SHARDS) + seat((owners >> 2) & (NZ - 1), owners & (NX - 1))
+    homes = owners // SHARDS
+    seats = seat((owners >> 2) & (NZ - 1), owners & (NX - 1))
     before = (homes[:, None] == homes[None, :]) & (owners[None, :] < owners[:, None])
-    slot = homes * RING + jnp.sum(before.astype(jnp.int32), axis=1)
+    slot = homes * SHARDS + jnp.sum(before.astype(jnp.int32), axis=1)
     order = jnp.sum(
-        jnp.where(slot[None, :] == jnp.arange(NY * RING, dtype=jnp.int32)[:, None], ids[None, :], 0), axis=1
+        jnp.where(slot[None, :] == jnp.arange(GROUPS * SHARDS, dtype=jnp.int32)[:, None], ids[None, :], 0), axis=1
     )
-    counts = jnp.sum((homes[None, :] == jnp.arange(NY, dtype=jnp.int32)[:, None]).astype(jnp.int32), axis=1)
+    counts = jnp.sum((homes[None, :] == jnp.arange(GROUPS, dtype=jnp.int32)[:, None]).astype(jnp.int32), axis=1)
     owned = jnp.any(owners == me)[None].astype(jnp.int32)
 
     blocks, following = muon_step(owned, rows, momentum[0].T)
-    blocks = lax.all_to_all(blocks, AXES, 0, 0, tiled=True, axis_index_groups=GROUPS_64)
-    few = 34
+    blocks = lax.all_to_all(blocks, AXES, 0, 0, tiled=True, axis_index_groups=MEMBERS)
+    few = 19
     updates = lax.cond(
         jnp.max(counts) <= few,
-        functools.partial(spread, few),
-        functools.partial(spread, RING),
+        functools.partial(spread, few, grads.shape),
+        functools.partial(spread, SHARDS, grads.shape),
         seats,
         order,
         counts,

time: 150 us -> 146 us (0.973)
  waiting for transfers between devices: 93 us -> 83.5 us
  starting transfers between devices: 30.8 us -> 36.1 us
    ppermute x13, starting transfers between devices: 13.5 us -> 20.4 us  [the longest x7 12.1 us: hop_core(): lax.ppermute(array, AXES, [(d, d ^ SHARDS) for d in range(GROUPS * SHARDS)])]
    ppermute x13, waiting for transfers between devices: 19.2 us -> 12.7 us  [the longest x6 12.7 us: hop_y(): lax.ppermute(array, AXES, [(d, (d + along * step) % count) for d in range...]
    all_to_all x2, waiting for transfers between devices: 73.8 us -> 70.8 us  [the longest x1 35.6 us: on_device(): lax.all_to_all(packed, AXES, 0, 0, tiled=True, axis_index_groups=MEMBERS)]
    all_to_all x2, starting transfers between devices: 17.3 us -> 15.6 us  [the longest x1 10.8 us: on_device(): lax.all_to_all(packed, AXES, 0, 0, tiled=True, axis_index_groups=MEMBERS)]
  transfers between devices with their start and end apart: 15 -> 15, of which waited for: 5 -> 6; matrix products, arithmetic and copies ran while one was open for 1% -> 1% of each run, Pallas kernels for 3% -> 3%
where the time goes in v1:
time: 146 us; the launch traced here: 145 us
  waiting for transfers between devices  83.5 us (57%)
  starting transfers between devices  36.1 us (25%)
  Pallas kernels  20.6 us (14%)
  between operations  2.19 us (2%)
  other arithmetic  1.69 us (1%)
    all_to_all x1, waiting for transfers between devices, on_device(): lax.all_to_all(packed, AXES, 0, 0, tiled=True, axis_index_groups=MEMBERS)  35.6 us
    all_to_all x1, waiting for transfers between devices, on_device(): lax.all_to_all(blocks, AXES, 0, 0, tiled=True, axis_index_groups=MEMBERS)  35.2 us
    ppermute x6, waiting for transfers between devices, hop_y(): lax.ppermute(array, AXES, [(d, (d + along * step) % count) for d in range...  12.7 us
    ppermute x7, starting transfers between devices, hop_core(): lax.ppermute(array, AXES, [(d, d ^ SHARDS) for d in range(GROUPS * SHARDS)])  12.1 us
    all_to_all x1, starting transfers between devices, on_device(): lax.all_to_all(packed, AXES, 0, 0, tiled=True, axis_index_groups=MEMBERS)  10.8 us
    pallas_call x2, Pallas kernels, place(): pl.pallas_call(functools.partial(place_kernel, origins), out_shape=jax.Sh...  8.87 us
    ppermute x6, starting transfers between devices, hop_y(): lax.ppermute(array, AXES, [(d, (d + along * step) % count) for d in range...  8.34 us
    pallas_call x1, Pallas kernels, muon_step(): pl.pallas_call(functools.partial(step_kernel, scale), out_shape=(jax.Shap...  7.27 us
  transfers between devices with their start and end apart: 15, of which 6 were waited for; matrix products, arithmetic and copies ran while one was open for 1% of the time, Pallas kernels for 3%

profile of v1, /device:TPU:33, one launch (start us, length us, event | category | flops | bytes accessed | tf_op | source)
XLA Modules:
  0.0 145.3 jit_solution(5280677341524601814)
XLA Ops:
  0.6 3.8 %pack_rows.1 = bf16[32,176,128]{2,1,0:T(8,128)(2,1)} custom-call(s32[104]{0:T(128)} %owners.1, s32[1]{0:T(128)} %bitcast.group, bf16[104,32,704]{2,1,0:T(8,128)(2,1)} %grads.1), custom_call_target="tpu_custom_call" | custom-call | tf_op jit(solution)/shard_map/pack_rows/pallas_call | solution.py:104
  4.4 0.0 copy-start.2
  4.5 10.8 %all-to-all-start = ((bf16[32,176,128]{2,1,0:T(8,128)(2,1)}), bf16[32,176,128]{2,1,0:T(8,128)(2,1)S(1)}, u32[]{:S(2)}, u32[]{:S(2)}) async-start(bf16[32,176,128]{2,1,0:T(8,128)(2,1)} %pack_rows.1), calls=%async_computation | async-start | bytes 2883584 | tf_op jit(solution)/shard_map/all_to_all | solution.py:294
  15.3 0.6 compare_reduce_fusion
  16.5 35.6 %all-to-all-done.rows_ref = bf16[32,176,128]{2,1,0:T(8,128)(2,1)S(1)} async-done(((bf16[32,176,128]{2,1,0:T(8,128)(2,1)}), bf16[32,176,128]{2,1,0:T(8,128)(2,1)S(1)}, u32[]{:S(2)}, u32[]{:S(2)}) %all-to-all-start) | async-done | bytes 1441824 | tf_op jit(solution)/shard_map/all_to_all | solution.py:294
  52.1 7.3 %newton_schulz.1 = (bf16[32,176,128]{2,1,0:T(8,128)(2,1)S(1)}, bf16[704,1024]{1,0:T(8,128)(2,1)}) custom-call(s32[1]{0:T(128)} %bitcast.1.owned_ref, bf16[32,176,128]{2,1,0:T(8,128)(2,1)S(1)} %all-to-all-done.rows_ref, bf16[704,1024]{1,0:T(8,128)(2,1)S(1)} %bitcast.8), custom_call_target="tpu_custom_call" | custom-call | tf_op jit(solution)/shard_map/newton_schulz/pallas_call | solution.py:174
  59.4 1.1 copy-done.1
  60.5 4.9 %all-to-all-start.1 = ((bf16[32,176,128]{2,1,0:T(8,128)(2,1)}), bf16[32,176,128]{2,1,0:T(8,128)(2,1)S(1)}, u32[]{:S(2)}, u32[]{:S(2)}) async-start(bf16[32,176,128]{2,1,0:T(8,128)(2,1)} %copy-done.1), calls=%async_computation.1 | async-start | bytes 2883584 | tf_op jit(solution)/shard_map/all_to_all | solution.py:308
  65.4 0.1 convert_reduce_fusion.1
  65.5 0.6 reduce_max.9
  66.8 0.2 convert_reduce_fusion
  67.0 0.1 select_reduce_fusion
  67.1 35.2 %all-to-all-done.1 = bf16[32,176,128]{2,1,0:T(8,128)(2,1)S(1)} async-done(((bf16[32,176,128]{2,1,0:T(8,128)(2,1)}), bf16[32,176,128]{2,1,0:T(8,128)(2,1)S(1)}, u32[]{:S(2)}, u32[]{:S(2)}) %all-to-all-start.1) | async-done | bytes 1441824 | tf_op jit(solution)/shard_map/all_to_all | solution.py:308
  102.3 42.8 %conditional.1 = (bf16[104,32,704]{2,1,0:T(8,128)(2,1)}) conditional(s32[]{:T(128)} %convert_element_type.15, (s32[104]{0:T(128)S(1)}, s32[256]{0:T(256)S(1)}, s32[8]{0:T(128)S(1)}, s32[1]{0:T(128)}, bf16[32,176,128]{2,1,0:T(8,128)(2,1)S(1)}) %tuple.16, (s32[104]{0:T(128)S(1)}, s32[256]{0:T(256)S(1)}, s32[8]{0:T(128)S(1)}, s32[1]{0:T(128)}, ...), branch_computations={%region_5.6_spmd, %region_6.7_spmd} | conditional | bytes 43254288 | solution.py:310
  102.3 0.7 select_blocks.3.refs_0_
  103.0 1.3 collective-permute-start.2
  104.4 1.6 %collective-permute-start.4 = (bf16[9,176,128]{2,1,0:T(8,128)(2,1)S(1)}, bf16[9,176,128]{2,1,0:T(8,128)(2,1)S(1)}, u32[]{:S(2)}, u32[]{:S(2)}) collective-permute-start(bf16[9,176,128]{2,1,0:T(8,128)(2,1)S(1)} %slice.14), channel_id=1, source_target_pairs={{0,192},{1,193},{2,194},{3,195},{4,196},{5,197},{6,198},{7,199},{8... | collective-permute-start | bytes 1216520 | tf_op jit(solution)/shard_map/cond/branch_1_fun/ppermute | solution.py:38
  106.0 2.6 %collective-permute-start.10 = (bf16[19,176,128]{2,1,0:T(8,128)(2,1)S(1)}, bf16[19,176,128]{2,1,0:T(8,128)(2,1)S(1)}, u32[]{:S(2)}, u32[]{:S(2)}) collective-permute-start(bf16[19,176,128]{2,1,0:T(8,128)(2,1)S(1)} %select_blocks.3.refs_0_), channel_id=1, source_target_pairs={{0,32},{1,33},{2,34},{3,35},{4,36},{5,37},{6,38},{7,39},{8,40},{9,... | collective-permute-start | bytes 2568200 | tf_op jit(solution)/shard_map/cond/branch_1_fun/ppermute | solution.py:42
  108.6 0.1 collective-permute-start
  108.7 2.6 %collective-permute-start.1 = (bf16[10,176,128]{2,1,0:T(8,128)(2,1)S(1)}, bf16[10,176,128]{2,1,0:T(8,128)(2,1)S(1)}, u32[]{:S(2)}, u32[]{:S(2)}) collective-permute-start(bf16[10,176,128]{2,1,0:T(8,128)(2,1)S(1)} %slice.15), channel_id=1, source_target_pairs={{0,192},{1,193},{2,194},{3,195},{4,196},{5,197},{6,198},{7,199},{8... | collective-permute-start | bytes 1351688 | tf_op jit(solution)/shard_map/cond/branch_1_fun/ppermute | solution.py:38
  111.3 3.0 %collective-permute-done.2.refs_1_ = bf16[10,176,128]{2,1,0:T(8,128)(2,1)S(1)} collective-permute-done((bf16[10,176,128]{2,1,0:T(8,128)(2,1)S(1)}, bf16[10,176,128]{2,1,0:T(8,128)(2,1)S(1)}, u32[]{:S(2)}, u32[]{:S(2)}) %collective-permute-start.2) | collective-permute-done | bytes 450592 | tf_op jit(solution)/shard_map/cond/branch_1_fun/ppermute | solution.py:38
  114.3 2.7 %collective-permute-start.5 = (bf16[9,176,128]{2,1,0:T(8,128)(2,1)S(1)}, bf16[9,176,128]{2,1,0:T(8,128)(2,1)S(1)}, u32[]{:S(2)}, u32[]{:S(2)}) collective-permute-start(bf16[9,176,128]{2,1,0:T(8,128)(2,1)S(1)} %collective-permute-done.4.refs_2_), channel_id=1, source_target_pairs={{0,192},{1,193},{2,194},{3,195},{4,196},{5,197},{6,198},{7,199},{8... | collective-permute-start | bytes 1216520 | tf_op jit(solution)/shard_map/cond/branch_1_fun/ppermute | solution.py:38
  116.9 6.0 %collective-permute-done.refs_0_ = bf16[9,176,128]{2,1,0:T(8,128)(2,1)S(1)} collective-permute-done((bf16[9,176,128]{2,1,0:T(8,128)(2,1)S(1)}, bf16[9,176,128]{2,1,0:T(8,128)(2,1)S(1)}, u32[]{:S(2)}, u32[]{:S(2)}) %collective-permute-start) | collective-permute-done | bytes 405536 | tf_op jit(solution)/shard_map/cond/branch_1_fun/ppermute | solution.py:38
  122.9 5.5 %collective-permute-start.12 = (bf16[9,176,128]{2,1,0:T(8,128)(2,1)S(1)}, bf16[9,176,128]{2,1,0:T(8,128)(2,1)S(1)}, u32[]{:S(2)}, u32[]{:S(2)}) collective-permute-start(bf16[9,176,128]{2,1,0:T(8,128)(2,1)S(1)} %collective-permute-done.4.refs_2_), channel_id=1, source_target_pairs={{0,32},{1,33},{2,34},{3,35},{4,36},{5,37},{6,38},{7,39},{8,40},{9,... | collective-permute-start | bytes 1216520 | tf_op jit(solution)/shard_map/cond/branch_1_fun/ppermute | solution.py:42
  128.4 0.5 collective-permute-start.11
  128.9 2.5 %collective-permute-done.5.refs_3_ = bf16[9,176,128]{2,1,0:T(8,128)(2,1)S(1)} collective-permute-done((bf16[9,176,128]{2,1,0:T(8,128)(2,1)S(1)}, bf16[9,176,128]{2,1,0:T(8,128)(2,1)S(1)}, u32[]{:S(2)}, u32[]{:S(2)}) %collective-permute-start.5) | collective-permute-done | bytes 405536 | tf_op jit(solution)/shard_map/cond/branch_1_fun/ppermute | solution.py:38
  131.4 1.2 collective-permute-done.3.refs_2_
  132.6 2.9 %collective-permute-start.7 = (bf16[10,176,128]{2,1,0:T(8,128)(2,1)S(1)}, bf16[10,176,128]{2,1,0:T(8,128)(2,1)S(1)}, u32[]{:S(2)}, u32[]{:S(2)}) collective-permute-start(bf16[10,176,128]{2,1,0:T(8,128)(2,1)S(1)} %collective-permute-done.1.refs_1_), channel_id=1, source_target_pairs={{0,32},{1,33},{2,34},{3,35},{4,36},{5,37},{6,38},{7,39},{8,40},{9,... | collective-permute-start | bytes 1351688 | tf_op jit(solution)/shard_map/cond/branch_1_fun/ppermute | solution.py:42
  135.5 0.5 collective-permute-start.6
  136.1 0.1 collective-permute-start.9
  136.2 4.7 %place_blocks.6.refs_8_ = bf16[104,32,704]{2,1,0:T(8,128)(2,1)} custom-call(s32[256]{0:T(256)S(1)} %get-tuple-element.32.order, s32[8]{0:T(128)S(1)} %get-tuple-element.33.counts, s32[1]{0:T(128)} %get-tuple-element.34.where, bf16[19,176,128]{2,1,0:T(8,128)(2,1)S(1)} %select_blocks.3.refs_0_, bf16[10,176,128]{2,1,0:T(8,128)(2,1)S(1)} %collective-permute-done.2.refs_1_, ...), custom_call_target="tpu_custom_call" | custom-call | tf_op jit(solution)/shard_map/cond/branch_1_fun/place_blocks/pallas_call | solution.py:256
  140.9 4.1 %place_blocks.7 = bf16[104,32,704]{2,1,0:T(8,128)(2,1)} custom-call(s32[256]{0:T(256)S(1)} %get-tuple-element.32.order, s32[8]{0:T(128)S(1)} %get-tuple-element.33.counts, s32[1]{0:T(128)} %get-tuple-element.34.where, bf16[9,176,128]{2,1,0:T(8,128)(2,1)S(1)} %collective-permute-done.refs_0_, ...), custom_call_target="tpu_custom_call", output_to_operand_aliasing={{}: (11, {})} | custom-call | tf_op jit(solution)/shard_map/cond/branch_1_fun/place_blocks/pallas_call | solution.py:256
  (19 shorter events, 0.1 us)
Async XLA Ops:
  4.4 10.8 %copy-start.2 = (s32[104]{0:T(128)S(1)}, s32[104]{0:T(128)}, u32[]{:S(2)}) copy-start(s32[104]{0:T(128)} %owners.1) | copy-start | bytes 1252
  4.5 47.7 %copy-start = (bf16[1,1024,704]{1,2,0:T(8,128)(2,1)S(1)}, bf16[1,1024,704]{1,2,0:T(8,128)(2,1)}, u32[]{:S(2)}) copy-start(bf16[1,1024,704]{1,2,0:T(8,128)(2,1)} %param.6) | copy-start | bytes 4325380
  4.5 47.7 %all-to-all-start = ((bf16[32,176,128]{2,1,0:T(8,128)(2,1)}), bf16[32,176,128]{2,1,0:T(8,128)(2,1)S(1)}, u32[]{:S(2)}, u32[]{:S(2)}) async-start(bf16[32,176,128]{2,1,0:T(8,128)(2,1)} %pack_rows.1), calls=%async_computation | async-start | bytes 2883584 | tf_op jit(solution)/shard_map/all_to_all | solution.py:294
  59.4 1.1 copy-start.1
  60.5 41.8 %all-to-all-start.1 = ((bf16[32,176,128]{2,1,0:T(8,128)(2,1)}), bf16[32,176,128]{2,1,0:T(8,128)(2,1)S(1)}, u32[]{:S(2)}, u32[]{:S(2)}) async-start(bf16[32,176,128]{2,1,0:T(8,128)(2,1)} %copy-done.1), calls=%async_computation.1 | async-start | bytes 2883584 | tf_op jit(solution)/shard_map/all_to_all | solution.py:308
  103.0 11.2 %collective-permute-start.2 = (bf16[10,176,128]{2,1,0:T(8,128)(2,1)S(1)}, bf16[10,176,128]{2,1,0:T(8,128)(2,1)S(1)}, u32[]{:S(2)}, u32[]{:S(2)}) collective-permute-start(bf16[10,176,128]{2,1,0:T(8,128)(2,1)S(1)} %slice.15), channel_id=1, source_target_pairs={{0,64},{1,65},{2,66},{3,67},{4,68},{5,69},{6,70},{7,71},{8,72},{9,... | collective-permute-start | bytes 1351688 | tf_op jit(solution)/shard_map/cond/branch_1_fun/ppermute | solution.py:38
  104.4 9.9 %collective-permute-start.4 = (bf16[9,176,128]{2,1,0:T(8,128)(2,1)S(1)}, bf16[9,176,128]{2,1,0:T(8,128)(2,1)S(1)}, u32[]{:S(2)}, u32[]{:S(2)}) collective-permute-start(bf16[9,176,128]{2,1,0:T(8,128)(2,1)S(1)} %slice.14), channel_id=1, source_target_pairs={{0,192},{1,193},{2,194},{3,195},{4,196},{5,197},{6,198},{7,199},{8... | collective-permute-start | bytes 1216520 | tf_op jit(solution)/shard_map/cond/branch_1_fun/ppermute | solution.py:38
  106.0 30.0 %collective-permute-start.10 = (bf16[19,176,128]{2,1,0:T(8,128)(2,1)S(1)}, bf16[19,176,128]{2,1,0:T(8,128)(2,1)S(1)}, u32[]{:S(2)}, u32[]{:S(2)}) collective-permute-start(bf16[19,176,128]{2,1,0:T(8,128)(2,1)S(1)} %select_blocks.3.refs_0_), channel_id=1, source_target_pairs={{0,32},{1,33},{2,34},{3,35},{4,36},{5,37},{6,38},{7,39},{8,40},{9,... | collective-permute-start | bytes 2568200 | tf_op jit(solution)/shard_map/cond/branch_1_fun/ppermute | solution.py:42
  108.6 14.3 %collective-permute-start = (bf16[9,176,128]{2,1,0:T(8,128)(2,1)S(1)}, bf16[9,176,128]{2,1,0:T(8,128)(2,1)S(1)}, u32[]{:S(2)}, u32[]{:S(2)}) collective-permute-start(bf16[9,176,128]{2,1,0:T(8,128)(2,1)S(1)} %slice.14), channel_id=1, source_target_pairs={{0,64},{1,65},{2,66},{3,67},{4,68},{5,69},{6,70},{7,71},{8,72},{9,... | collective-permute-start | bytes 1216520 | tf_op jit(solution)/shard_map/cond/branch_1_fun/ppermute | solution.py:38
  108.7 19.8 %collective-permute-start.1 = (bf16[10,176,128]{2,1,0:T(8,128)(2,1)S(1)}, bf16[10,176,128]{2,1,0:T(8,128)(2,1)S(1)}, u32[]{:S(2)}, u32[]{:S(2)}) collective-permute-start(bf16[10,176,128]{2,1,0:T(8,128)(2,1)S(1)} %slice.15), channel_id=1, source_target_pairs={{0,192},{1,193},{2,194},{3,195},{4,196},{5,197},{6,198},{7,199},{8... | collective-permute-start | bytes 1351688 | tf_op jit(solution)/shard_map/cond/branch_1_fun/ppermute | solution.py:38
  114.2 18.3 %collective-permute-start.3 = (bf16[10,176,128]{2,1,0:T(8,128)(2,1)S(1)}, bf16[10,176,128]{2,1,0:T(8,128)(2,1)S(1)}, u32[]{:S(2)}, u32[]{:S(2)}) collective-permute-start(bf16[10,176,128]{2,1,0:T(8,128)(2,1)S(1)} %collective-permute-done.2.refs_1_), channel_id=1, source_target_pairs={{0,64},{1,65},{2,66},{3,67},{4,68},{5,69},{6,70},{7,71},{8,72},{9,... | collective-permute-start | bytes 1351688 | tf_op jit(solution)/shard_map/cond/branch_1_fun/ppermute | solution.py:38
  114.3 17.1 %collective-permute-start.5 = (bf16[9,176,128]{2,1,0:T(8,128)(2,1)S(1)}, bf16[9,176,128]{2,1,0:T(8,128)(2,1)S(1)}, u32[]{:S(2)}, u32[]{:S(2)}) collective-permute-start(bf16[9,176,128]{2,1,0:T(8,128)(2,1)S(1)} %collective-permute-done.4.refs_2_), channel_id=1, source_target_pairs={{0,192},{1,193},{2,194},{3,195},{4,196},{5,197},{6,198},{7,199},{8... | collective-permute-start | bytes 1216520 | tf_op jit(solution)/shard_map/cond/branch_1_fun/ppermute | solution.py:38
  122.9 12.6 %collective-permute-start.12 = (bf16[9,176,128]{2,1,0:T(8,128)(2,1)S(1)}, bf16[9,176,128]{2,1,0:T(8,128)(2,1)S(1)}, u32[]{:S(2)}, u32[]{:S(2)}) collective-permute-start(bf16[9,176,128]{2,1,0:T(8,128)(2,1)S(1)} %collective-permute-done.4.refs_2_), channel_id=1, source_target_pairs={{0,32},{1,33},{2,34},{3,35},{4,36},{5,37},{6,38},{7,39},{8,40},{9,... | collective-permute-start | bytes 1216520 | tf_op jit(solution)/shard_map/cond/branch_1_fun/ppermute | solution.py:42
  128.4 7.7 %collective-permute-start.11 = (bf16[10,176,128]{2,1,0:T(8,128)(2,1)S(1)}, bf16[10,176,128]{2,1,0:T(8,128)(2,1)S(1)}, u32[]{:S(2)}, u32[]{:S(2)}) collective-permute-start(bf16[10,176,128]{2,1,0:T(8,128)(2,1)S(1)} %collective-permute-done.2.refs_1_), channel_id=1, source_target_pairs={{0,32},{1,33},{2,34},{3,35},{4,36},{5,37},{6,38},{7,39},{8,40},{9,... | collective-permute-start | bytes 1351688 | tf_op jit(solution)/shard_map/cond/branch_1_fun/ppermute | solution.py:42
  132.6 8.3 %collective-permute-start.7 = (bf16[10,176,128]{2,1,0:T(8,128)(2,1)S(1)}, bf16[10,176,128]{2,1,0:T(8,128)(2,1)S(1)}, u32[]{:S(2)}, u32[]{:S(2)}) collective-permute-start(bf16[10,176,128]{2,1,0:T(8,128)(2,1)S(1)} %collective-permute-done.1.refs_1_), channel_id=1, source_target_pairs={{0,32},{1,33},{2,34},{3,35},{4,36},{5,37},{6,38},{7,39},{8,40},{9,... | collective-permute-start | bytes 1351688 | tf_op jit(solution)/shard_map/cond/branch_1_fun/ppermute | solution.py:42
  135.5 5.4 %collective-permute-start.8 = (bf16[10,176,128]{2,1,0:T(8,128)(2,1)S(1)}, bf16[10,176,128]{2,1,0:T(8,128)(2,1)S(1)}, u32[]{:S(2)}, u32[]{:S(2)}) collective-permute-start(bf16[10,176,128]{2,1,0:T(8,128)(2,1)S(1)} %collective-permute-done.3.refs_2_), channel_id=1, source_target_pairs={{0,32},{1,33},{2,34},{3,35},{4,36},{5,37},{6,38},{7,39},{8,40},{9,... | collective-permute-start | bytes 1351688 | tf_op jit(solution)/shard_map/cond/branch_1_fun/ppermute | solution.py:42
  135.5 5.4 %collective-permute-start.6 = (bf16[9,176,128]{2,1,0:T(8,128)(2,1)S(1)}, bf16[9,176,128]{2,1,0:T(8,128)(2,1)S(1)}, u32[]{:S(2)}, u32[]{:S(2)}) collective-permute-start(bf16[9,176,128]{2,1,0:T(8,128)(2,1)S(1)} %collective-permute-done.refs_0_), channel_id=1, source_target_pairs={{0,32},{1,33},{2,34},{3,35},{4,36},{5,37},{6,38},{7,39},{8,40},{9,... | collective-permute-start | bytes 1216520 | tf_op jit(solution)/shard_map/cond/branch_1_fun/ppermute | solution.py:42
  136.1 4.9 %collective-permute-start.9 = (bf16[9,176,128]{2,1,0:T(8,128)(2,1)S(1)}, bf16[9,176,128]{2,1,0:T(8,128)(2,1)S(1)}, u32[]{:S(2)}, u32[]{:S(2)}) collective-permute-start(bf16[9,176,128]{2,1,0:T(8,128)(2,1)S(1)} %collective-permute-done.5.refs_3_), channel_id=1, source_target_pairs={{0,32},{1,33},{2,34},{3,35},{4,36},{5,37},{6,38},{7,39},{8,40},{9,... | collective-permute-start | bytes 1216520 | tf_op jit(solution)/shard_map/cond/branch_1_fun/ppermute | solution.py:42
